TPU v7x, 256 devices: a whole 4x4x8 slice. The times are simulated.
256 devices in a mesh: row: 32 (over x, z_lo, core), col: 8 (over z_hi, y).
Axes of the slice: x: 4, y: 4, z: 8 (z_hi: 2, z_lo: 4; z = z_hi * 4 + z_lo), core: 2. Of those that a mesh axis runs over, the one named last changes fastest.
Arguments:
- inverse_anc: float32 [8192, 8192], P('row', 'col'), as said below
- lower_panel: float32 [8192, 2048], P('row', 'col'), may hold values from -0.5 to 0.5
- structure: int32 [8, 16], P('col'), may hold values from 0 to 31, as said below
- diag_inverse: float32 [2048, 256], P('col'), may hold values from -6 to 6
Outputs:
- inverse_panel: float32 [8192, 2048], P('row', 'col')
- diagonal_block: float32 [2048, 256], P('col')
Inputs may be any that keep to these rules, and one draw needn't show every extreme that they name: inverse_anc is exactly symmetric. `structure`: each row lists 16 different ancestor block numbers in increasing order; each index of col holds exactly one row (one lower supernode).
All inputs are finite; a program needn't handle non-finite values.
Results may differ from a plain program's by a relative error of at most 0.000075.
Values sent between devices are 32-bit elements; how exact they have to be, the bound alone decides.
A program may use at most 64 MiB of HBM per device.

v0:
```python
import jax
import jax.numpy as jnp
from jax import lax
from jax.sharding import PartitionSpec as P


def keep_rows(structure, first_row, row_count, sn_width):
    block_ids = (first_row + jnp.arange(row_count, dtype=jnp.int32)) // sn_width
    listed = jnp.any(structure[None, :, :] == block_ids[:, None, None], axis=2)
    return jnp.repeat(listed, sn_width, axis=1)


def local(inverse_anc, lower_panel, structure, diag_inverse):
    local_rows = inverse_anc.shape[0]
    sn_width = diag_inverse.shape[1]
    local_count = structure.shape[0]
    first_local = lax.axis_index("row") * local_rows
    keep_local = keep_rows(structure, first_local, local_rows, sn_width)
    masked = jnp.where(keep_local, lower_panel, jnp.float32(0.0))
    strip = lax.all_gather(inverse_anc, "col", axis=1, tiled=True)
    product = lax.psum_scatter(
        lax.dot_general(
            strip,
            masked,
            (((0,), (0,)), ((), ())),
            precision=lax.Precision.HIGHEST,
            preferred_element_type=jnp.float32,
        ),
        "row",
        scatter_dimension=0,
        tiled=True,
    )
    panel = jnp.where(keep_local, -product, jnp.float32(0.0))
    lower_blocks = masked.reshape(local_rows, local_count, sn_width)
    panel_blocks = panel.reshape(local_rows, local_count, sn_width)
    partial_value = jnp.einsum(
        "ika,ikb->kab", lower_blocks, panel_blocks, precision=lax.Precision.HIGHEST
    )
    diag_sum = lax.psum(partial_value.reshape(local_count * sn_width, sn_width), "row")
    return (panel, diag_inverse - diag_sum)


def solution(mesh):
    placed = (P("row", "col"), P("row", "col"), P("col", None), P("col", None))
    return jax.shard_map(
        local,
        mesh=mesh,
        in_specs=placed,
        out_specs=(P("row", "col"), P("col", None)),
        check_vma=False,
    )
```

profile of v0, /device:TPU:1, one launch (start us, length us, event | category | flops | bytes accessed | tf_op | source)
XLA Modules:
  0.0 638.4 jit_solution(457887410385714757)
XLA Ops:
  7.2 0.0 all-gather.2.cloned.1.call-start
  7.2 0.7 all-gather.2.cloned.1.call-update
  7.9 0.0 reduce-scatter.2.cloned.1.call-start
  7.9 1.1 copy.8
  9.1 0.7 compare_reduce_fusion
  9.8 177.6 %all-gather.2.cloned.1.call-done = f32[256,8192]{1,0:T(8,128)} async-done(((f32[256,1024]{1,0:T(8,128)}), f32[256,8192]{1,0:T(8,128)}) %all-gather.2.cloned.1.call-update) | async-done | bytes 8388624 | tf_op jit(solution)/shard_map/all_gather | solution.py:20
  187.4 11.7 %convolution_bitcast_fusion = f32[8192,256]{0,1:T(8,128)} fusion(f32[256,8192]{1,0:T(8,128)} %all-gather.2.cloned.1.call-done, f32[256,256]{0,1:T(8,128)S(1)} %copy.8, pred[256]{0:T(512)(128)(4,1)S(1)} %compare_reduce_fusion), kind=kOutput, calls=%fused_computation | convolution fusion | flops 6442516480 | bytes 17039616 | tf_op jit(solution)/shard_map/dot_general | solution.py:22
  199.1 0.0 copy-start
  199.1 0.0 reduce-scatter.2.cloned.1.call-update
  199.1 0.0 all-reduce.2.cloned.1.call-start
  199.1 153.2 %reduce-scatter.2.cloned.1.call-done = f32[256,256]{0,1:T(8,128)} async-done(((f32[8192,256]{0,1:T(8,128)}), f32[256,256]{0,1:T(8,128)}) %reduce-scatter.2.cloned.1.call-update) | async-done | bytes 262160 | tf_op jit(solution)/shard_map/reduce_scatter | solution.py:21
  352.4 2.1 fusion
  354.4 0.0 all-reduce.2.cloned.1.call-update
  354.5 1.0 negate_select_fusion
  355.4 0.8 copy.9
  356.3 273.9 %all-reduce.2.cloned.1.call-done = f32[256,256]{1,0:T(8,128)} async-done(((f32[256,256]{1,0:T(8,128)}), f32[256,256]{1,0:T(8,128)}) %all-reduce.2.cloned.1.call-update) | async-done | bytes 262160 | tf_op jit(solution)/shard_map/psum | solution.py:39
  630.2 0.0 copy-done
  630.2 1.7 sub.10
  (1 shorter events, 0.0 us)
Async XLA Ops:
  7.2 180.2 %all-gather.2.cloned.1.call-start = ((), (), s32[]{:S(2)}) async-start(), calls=%async_computation.1 | async-start | bytes 9437184 | tf_op jit(solution)/shard_map/all_gather | solution.py:20
  7.9 344.5 %reduce-scatter.2.cloned.1.call-start = ((), (), s32[]{:S(2)}) async-start(), calls=%async_computation.2 | async-start | bytes 8650752 | tf_op jit(solution)/shard_map/reduce_scatter | solution.py:21
  199.1 431.1 %copy-start = (f32[256,256]{1,0:T(8,128)S(1)}, f32[256,256]{1,0:T(8,128)}, u32[]{:S(2)}) copy-start(f32[256,256]{1,0:T(8,128)} %param.7) | copy-start | bytes 786436
  199.1 431.1 %all-reduce.2.cloned.1.call-start = ((), (), s32[]{:S(2)}) async-start(), calls=%async_computation.3 | async-start | bytes 524288 | tf_op jit(solution)/shard_map/psum | solution.py:39
Sparse Core Ops, SparseCore 0:
  10.6 176.7 all-gather.1
  199.2 153.1 reduce-scatter.1
  355.6 274.5 all-reduce.1
where the time goes:
time: 639 us; the launch traced here: 638 us
  waiting for transfers between devices  605 us (95%)
  between operations  13.8 us (2%)
  matrix products  13.7 us (2%)
    psum x1, waiting for transfers between devices, local(): lax.psum(partial_value.reshape(local_count * sn_width, sn_width), 'row')  274 us
    all_gather x1, waiting for transfers between devices, local(): strip = lax.all_gather(inverse_anc, 'col', axis=1, tiled=True)  178 us
    reduce_scatter x1, waiting for transfers between devices, local(): lax.psum_scatter(lax.dot_general(strip, masked, (((0,), (0,)), ((), ())),...  153 us
  transfers between devices with their start and end apart: 3, of which 3 were waited for; matrix products, arithmetic and copies ran while one was open for 1% of the time, Pallas kernels for 0%

commit v1 on v0

v1 whole, which is shorter than its diff:
```python
import functools

import jax
import jax.numpy as jnp
from jax import lax
from jax.experimental import pallas as pl
from jax.experimental.pallas import tpu as pltpu
from jax.sharding import PartitionSpec as P

MESH = pl.DeviceIdType.MESH
Q = 2
W = 128
B = 256


def device(x, zl, core, zh, y):
    return ((x * 4 + zl) * 2 + core, zh * 4 + y)


def slot_of(zl, same):
    high = zl // 2
    return same * zl + (1 - same) * (high * (3 - zl) + (1 - high) * (2 + zl))


def split(value):
    high = value.astype(jnp.bfloat16)
    return high, (value - high.astype(jnp.float32)).astype(jnp.bfloat16)


def dot3(a_high, a_low, b_high, b_low):
    dot = functools.partial(jnp.dot, preferred_element_type=jnp.float32)
    return dot(a_high, b_high) + (dot(a_high, b_low) + dot(a_low, b_high))


def kernel(
    a_ref, m_ref, st_ref, dinv_ref, p_ref, d_ref,
    a_own, a_other, a_hi, a_lo, m_in, m_own, mt_hi, mt_lo, m_all, m_hi, m_lo,
    part, c1, c2, nf, t_buf, t_in, t_out,
    load_sem, a_sem, home_s, home_r, z_s, z_r, x_s, x_r, f_s, f_r,
    c1_s, c1_r, c2_s, c2_r, n_s, n_r, fz_s, fz_r, t_s, t_r, o_s, o_r,
):
    row = lax.axis_index("row")
    col = lax.axis_index("col")
    x, zl, core = row // 8, (row // 2) % 4, row % 2
    zh, y = col // 4, col % 4

    load_m = pltpu.make_async_copy(m_ref, m_in, load_sem.at[0])
    load_m.start()
    load_a = pltpu.make_async_copy(a_ref, a_own, load_sem.at[1])
    load_a.start()

    b = zl % 2
    to_zh, to_y = x // 2, (x % 2) * 2 + zl // 2
    same = 1 - (zh - to_zh) * (zh - to_zh)
    to_x = (y + x) % 4
    to_zl = same * (2 * b + core) + (1 - same) * ((1 - b) * (3 - core) + b * core)
    off = (
        (to_x - x) * (to_x - x) + (to_zl - zl) * (to_zl - zl) + (zh - core) * (zh - core)
        + (to_zh - zh) * (to_zh - zh) + (to_y - y) * (to_y - y)
    )
    home = device(to_x, to_zl, zh, to_zh, to_y)
    from_x = 2 * zh + y // 2
    same_half = 1 - (core - zh) * (core - zh)
    j4 = slot_of(zl, same_half)
    from_y = (x - from_x + 4) % 4
    source = device(from_x, 2 * (y % 2) + j4 // 2, j4 % 2, core, from_y)

    far = (core - zh) * (core - zh)
    right_y, left_y = (y + 1) % 4, (y + 3) % 4

    barrier = pltpu.get_barrier_semaphore()

    def greet(d, carry):
        pl.semaphore_signal(barrier, inc=1, device_id=((row + d) % 32, col), device_id_type=MESH)
        return carry

    lax.fori_loop(1, 32, greet, 0)
    pl.semaphore_signal(barrier, inc=1, device_id=(row, zh * 4 + right_y), device_id_type=MESH)
    pl.semaphore_signal(barrier, inc=1, device_id=(row, zh * 4 + left_y), device_id_type=MESH)
    pl.semaphore_signal(barrier, inc=1, device_id=device(x, zl, zh, 1 - zh, y), device_id_type=MESH)

    @pl.when(off > 0)
    def _():
        pl.semaphore_signal(barrier, inc=1, device_id=source, device_id_type=MESH)

    listed = st_ref[0, 0] == row
    for s in range(1, 16):
        listed = listed | (st_ref[0, s] == row)
    keep = jnp.where(listed, 1, 0)
    load_m.wait()
    masked = jnp.where(jnp.broadcast_to(keep, (B, B)) > 0, m_in[...], 0.0)
    for q in range(Q):
        m_own[q] = masked[:, q * W:(q + 1) * W]

    pl.semaphore_wait(barrier, 33 + 2 * far + jnp.minimum(off, 1))

    def remote(src, dst, send, recv, target):
        return pltpu.make_async_remote_copy(
            src_ref=src, dst_ref=dst, send_sem=send, recv_sem=recv,
            device_id=target, device_id_type=MESH,
        )

    own_slot = 2 * b + core
    sends = []
    for q in range(Q):
        @pl.when(off > 0)
        def _(q=q):
            remote(m_own.at[q], m_all.at[q, own_slot, y], home_s.at[q], home_r.at[q], home).start()

        @pl.when(off == 0)
        def _(q=q):
            pltpu.make_async_copy(m_own.at[q], m_all.at[q, own_slot, y], home_r.at[q]).start()

    a_copy = remote(a_ref, a_other, a_sem.at[0], a_sem.at[1], device(x, zl, 1 - core, zh, y))
    a_copy.start()

    mt_hi[...], mt_lo[...] = split(masked.T)

    load_a.wait()
    hi, lo = split(a_own[...])
    a_hi[core], a_lo[core] = hi, lo

    def unit(q, h, at_x):
        return m_all.at[q, slot_of(h, same_half), (at_x - from_x + 8) % 4]

    def z_send(q):
        for i, d in enumerate((1, 3, 2)):
            cp = remote(unit(q, zl, x), unit(q, zl, x), z_s.at[q, i], z_r.at[q, zl],
                        device(x, (zl + d) % 4, core, zh, y))
            cp.start()
            sends.append(cp)

    def x_send(q, h):
        for i, d in enumerate((1, 3)):
            cp = remote(unit(q, h, x), unit(q, h, x), x_s.at[q, h, i], x_r.at[q, h, i],
                        device((x + d) % 4, zl, core, zh, y))
            cp.start()
            sends.append(cp)

    def x_wait(q, h, i):
        src = unit(q, h, x + (3 if i == 0 else 1))
        remote(src, src, x_s.at[q, h, i], x_r.at[q, h, i], device((x + 1) % 4, zl, core, zh, y)).wait_recv()

    def home_wait(q):
        u = unit(q, zl, x)
        pltpu.make_async_copy(u, u, home_r.at[q]).wait()

    order = (0, 1, 3, 2)

    def forward(q, h, i):
        u = unit(q, h, x + (3 if i == 0 else 1))
        cp = remote(u, u, f_s.at[q, h], f_r.at[q, h],
                    device((x + (1 if i == 0 else 3)) % 4, zl, core, zh, y))
        cp.start()
        sends.append(cp)

    def x_sends(q):
        x_send(q, zl)
        for d in order[1:]:
            h = (zl + d) % 4
            u = unit(q, h, x)
            remote(u, u, z_s.at[q, 0], z_r.at[q, h], device(x, (zl + 1) % 4, core, zh, y)).wait_recv()
            x_send(q, h)

    def forwards(q):
        for h in range(4):
            x_wait(q, h, h % 2)
            forward(q, h, h % 2)

    def gathered(q):
        for h in range(4):
            x_wait(q, h, 1 - h % 2)
        for h in range(4):
            u = unit(q, h, x + 2)
            remote(u, u, f_s.at[q, h], f_r.at[q, h], device((x + 1) % 4, zl, core, zh, y)).wait_recv()

    def multiply(q):
        for j in range(4):
            for k in range(4):
                hi, lo = split(m_all[q, j, k])
                m_hi[j * B:(j + 1) * B, k * W:(k + 1) * W] = hi
                m_lo[j * B:(j + 1) * B, k * W:(k + 1) * W] = lo
        for r in range(2):
            out = dot3(a_hi[r], a_lo[r], m_hi[...], m_lo[...])
            for k in range(4):
                part[q, k, r] = out[:, k * W:(k + 1) * W]

    def to_right(src, dst, send, recv):
        cp = remote(src, dst, send, recv, (row, zh * 4 + right_y))
        cp.start()
        sends.append(cp)

    def to_left(src, dst, send, recv):
        cp = remote(src, dst, send, recv, (row, zh * 4 + left_y))
        cp.start()
        sends.append(cp)

    def scatter_first(q):
        over = (y + 2) % 4
        to_right(part.at[q, over, 0], c1.at[q, 0], c1_s.at[q, 0], c1_r.at[q, 0])
        to_left(part.at[q, over, 1], c1.at[q, 1], c1_s.at[q, 1], c1_r.at[q, 1])
        to_right(part.at[q, right_y, 1], c2.at[q, 0, 1], c2_s.at[q, 0, 1], c2_r.at[q, 0, 1])
        to_left(part.at[q, left_y, 0], c2.at[q, 1, 0], c2_s.at[q, 1, 0], c2_r.at[q, 1, 0])

    def arrived(buf, send, recv):
        remote(buf, buf, send, recv, (row, zh * 4 + right_y)).wait_recv()

    def scatter_second(q):
        arrived(c1.at[q, 0], c1_s.at[q, 0], c1_r.at[q, 0])
        part[q, right_y, 0] = part[q, right_y, 0] + c1[q, 0]
        to_right(part.at[q, right_y, 0], c2.at[q, 0, 0], c2_s.at[q, 0, 0], c2_r.at[q, 0, 0])
        arrived(c1.at[q, 1], c1_s.at[q, 1], c1_r.at[q, 1])
        part[q, left_y, 1] = part[q, left_y, 1] + c1[q, 1]
        to_left(part.at[q, left_y, 1], c2.at[q, 1, 1], c2_s.at[q, 1, 1], c2_r.at[q, 1, 1])

    def scatter_last(q):
        for r in range(2):
            for i in range(2):
                arrived(c2.at[q, i, r], c2_s.at[q, i, r], c2_r.at[q, i, r])
        for r in range(2):
            part[q, y, r] = part[q, y, r] + (c2[q, 0, r] + c2[q, 1, r])

        @pl.when(far == 0)
        def _():
            remote(part.at[q, y, 1 - core], nf.at[q, 0], n_s.at[q], n_r.at[q],
                   device(x, zl, 1 - core, zh, y)).start()
            nf[q, 0] = part[q, y, core]

        @pl.when(far == 1)
        def _():
            for r in range(2):
                remote(part.at[q, y, r], nf.at[q, 1], fz_s.at[q, r], fz_r.at[q],
                       device(x, zl, r, 1 - zh, y)).start()

    def finish(q):
        @pl.when(far == 1)
        def _():
            arrived(nf.at[q, 0], n_s.at[q], n_r.at[q])

        arrived(nf.at[q, 1], fz_s.at[q, 0], fz_r.at[q])
        panel = jnp.where(jnp.broadcast_to(keep, (B, W)) > 0, -(nf[q, 0] + nf[q, 1]), 0.0)
        p_ref[:, q * W:(q + 1) * W] = panel
        p_hi, p_lo = split(panel)
        t_buf[:, :, q * W:(q + 1) * W] = dot3(mt_hi[...], mt_lo[...], p_hi, p_lo).reshape(32, 8, W)

    home_wait(0)
    z_send(0)
    home_wait(1)
    z_send(1)
    x_sends(0)
    a_copy.wait()
    hi, lo = split(a_other[...])
    a_hi[1 - core], a_lo[1 - core] = hi, lo
    forwards(0)
    x_sends(1)
    gathered(0)
    multiply(0)
    scatter_first(0)
    forwards(1)
    scatter_second(0)
    scatter_last(0)
    gathered(1)
    multiply(1)
    scatter_first(1)
    scatter_second(1)
    finish(0)
    scatter_last(1)
    finish(1)

    def t_copy(d):
        peer = (row + d) % 32
        return remote(t_buf.at[peer], t_in.at[row], t_s.at[d], t_r.at[0], (peer, col))

    def o_copy(d):
        peer = (row + d) % 32
        return remote(t_out.at[row], t_out.at[row], o_s.at[d], o_r.at[0], (peer, col))

    def start(copy):
        def body(d, carry):
            copy(d).start()
            return carry
        lax.fori_loop(1, 32, body, 0)

    start(t_copy)
    t_in[row] = t_buf[row]
    every = t_in.at[pl.ds(0, 31)]
    remote(every, every, t_s.at[0], t_r.at[0], ((row + 1) % 32, col)).wait_recv()
    total = jnp.sum(t_in[...], axis=0)
    first = pl.multiple_of(row * 8, 8)
    t_out[row] = dinv_ref[pl.ds(first, 8), :] - total
    start(o_copy)
    every = t_out.at[pl.ds(0, 31)]
    remote(every, every, o_s.at[0], o_r.at[0], ((row + 1) % 32, col)).wait_recv()
    d_ref[...] = t_out[...].reshape(B, B)

    for cp in sends:
        cp.wait_send()
    for q in range(Q):
        @pl.when(off > 0)
        def _(q=q):
            remote(m_own.at[q], m_all.at[q, own_slot, y], home_s.at[q], home_r.at[q], home).wait_send()

        @pl.when(far == 0)
        def _(q=q):
            remote(part.at[q, y, 1 - core], nf.at[q, 0], n_s.at[q], n_r.at[q],
                   device(x, zl, 1 - core, zh, y)).wait_send()

        @pl.when(far == 1)
        def _(q=q):
            for r in range(2):
                remote(part.at[q, y, r], nf.at[q, 1], fz_s.at[q, r], fz_r.at[q],
                       device(x, zl, r, 1 - zh, y)).wait_send()

    def left(d, carry):
        t_copy(d).wait_send()
        o_copy(d).wait_send()
        return carry

    lax.fori_loop(1, 32, left, 0)


def local(inverse_anc, lower_panel, structure, diag_inverse):
    f32, bf16 = jnp.float32, jnp.bfloat16
    dma = pltpu.SemaphoreType.DMA
    hbm = pl.BlockSpec(memory_space=pl.ANY)
    vmem = pl.BlockSpec(memory_space=pltpu.VMEM)
    return pl.pallas_call(
        kernel,
        out_shape=(jax.ShapeDtypeStruct((B, B), f32), jax.ShapeDtypeStruct((B, B), f32)),
        in_specs=[hbm, hbm, pl.BlockSpec(memory_space=pltpu.SMEM), vmem],
        out_specs=(vmem, vmem),
        scratch_shapes=[
            pltpu.VMEM((B, 4 * B), f32), pltpu.VMEM((B, 4 * B), f32),
            pltpu.VMEM((2, B, 4 * B), bf16), pltpu.VMEM((2, B, 4 * B), bf16),
            pltpu.VMEM((B, B), f32), pltpu.VMEM((Q, B, W), f32),
            pltpu.VMEM((B, B), bf16), pltpu.VMEM((B, B), bf16),
            pltpu.VMEM((Q, 4, 4, B, W), f32),
            pltpu.VMEM((4 * B, 4 * W), bf16), pltpu.VMEM((4 * B, 4 * W), bf16),
            pltpu.VMEM((Q, 4, 2, B, W), f32),
            pltpu.VMEM((Q, 2, B, W), f32), pltpu.VMEM((Q, 2, 2, B, W), f32),
            pltpu.VMEM((Q, 2, B, W), f32),
            pltpu.VMEM((32, 8, B), f32), pltpu.VMEM((32, 8, B), f32), pltpu.VMEM((32, 8, B), f32),
            dma((2,)), dma((2,)), dma((Q,)), dma((Q,)), dma((Q, 3)), dma((Q, 4)),
            dma((Q, 4, 2)), dma((Q, 4, 2)), dma((Q, 4)), dma((Q, 4)),
            dma((Q, 2)), dma((Q, 2)), dma((Q, 2, 2)), dma((Q, 2, 2)),
            dma((Q,)), dma((Q,)), dma((Q, 2)), dma((Q,)),
            dma((32,)), dma((1,)), dma((32,)), dma((1,)),
        ],
        compiler_params=pltpu.CompilerParams(
            collective_id=0, has_side_effects=True, vmem_limit_bytes=48 * 2**20
        ),
    )(inverse_anc, lower_panel, structure, diag_inverse)


def solution(mesh):
    placed = (P("row", "col"), P("row", "col"), P("col", None), P("col", None))
    return jax.shard_map(
        local,
        mesh=mesh,
        in_specs=placed,
        out_specs=(P("row", "col"), P("col", None)),
        check_vma=False,
    )
```

time: 639 us -> 108 us (0.17)
  waiting for transfers between devices: 605 us -> 0 us
  Pallas kernels: 0 us -> 102 us
  matrix products: 13.7 us -> 0 us
  between operations: 13.8 us -> 0.65 us
    psum x1 -> x0, waiting for transfers between devices: 274 us -> none  [local(): lax.psum(partial_value.reshape(local_count * sn_width, sn_width), 'row')]
    all_gather x1 -> x0, waiting for transfers between devices: 178 us -> none  [local(): strip = lax.all_gather(inverse_anc, 'col', axis=1, tiled=True)]
    reduce_scatter x1 -> x0, waiting for transfers between devices: 153 us -> none  [local(): lax.psum_scatter(lax.dot_general(strip, masked, (((0,), (0,)), ((), ())),...]
    pallas_call x0 -> x1, Pallas kernels: none -> 102 us  [local(): pl.pallas_call(kernel, out_shape=(jax.ShapeDtypeStruct((B, B), f32), jax....]
    dot_general x2 -> x0, matrix products: 13.7 us -> none  [the longest x1 11.7 us: local(): lax.dot_general(strip, masked, (((0,), (0,)), ((), ())), precision=lax.Pr...]
  transfers between devices with their start and end apart: 3 -> 0, of which waited for: 3 -> 0; matrix products, arithmetic and copies ran while one was open for 1% -> 0% of each run, Pallas kernels for 0% -> 0%
where the time goes in v1:
time: 108 us
  Pallas kernels  102 us (94%)
  local copies, waits for them, and re-layouts  5.18 us (5%)
    pallas_call x1, Pallas kernels, local(): pl.pallas_call(kernel, out_shape=(jax.ShapeDtypeStruct((B, B), f32), jax....  102 us
    unnamed x10, local copies, waits for them, and re-layouts  5.18 us

profile of v1, /device:TPU:1, one launch (start us, length us, event | category | flops | bytes accessed | tf_op | source)
XLA Modules:
  0.0 108.0 jit_solution(8878855823001139421)
XLA Ops:
  0.6 0.0 copy-start
  0.6 1.2 %copy-done = f32[256,1024]{1,0:T(8,128)S(1)} copy-done((f32[256,1024]{1,0:T(8,128)S(1)}, f32[256,1024]{1,0:T(8,128)}, u32[]{:S(2)}) %copy-start) | copy-done | bytes 1048600
  1.9 0.0 copy-start.1
  1.9 0.9 copy-done.1
  2.8 0.0 copy-start.2
  2.8 0.9 copy-done.2
  3.8 0.0 copy-start.3
  3.8 0.7 copy-done.3
  4.4 102.2 %shard_map.59 = (f32[256,256]{1,0:T(8,128)S(1)}, f32[256,256]{1,0:T(8,128)S(1)}) custom-call(f32[256,1024]{1,0:T(8,128)S(1)} %copy-done, f32[256,256]{1,0:T(8,128)S(1)} %copy-done.1, s32[1,16]{1,0:T(1,128)S(1)} %copy-done.3, f32[256,256]{1,0:T(8,128)S(1)} %copy-done.2), custom_call_target="tpu_custom_call" | custom-call | tf_op jit(solution)/shard_map/pallas_call | solution.py:327
  106.6 0.7 copy.8
  107.3 0.7 copy.9
Async XLA Ops:
  0.6 1.2 %copy-start = (f32[256,1024]{1,0:T(8,128)S(1)}, f32[256,1024]{1,0:T(8,128)}, u32[]{:S(2)}) copy-start(f32[256,1024]{1,0:T(8,128)} %a_ref.1) | copy-start | bytes 3145732
  1.9 0.9 copy-start.1
  2.8 0.9 copy-start.2
  3.8 0.7 copy-start.3

commit v2 on v0

v2 whole, which is shorter than its diff:
```python
import functools

import jax
import jax.numpy as jnp
from jax import lax
from jax.experimental import pallas as pl
from jax.experimental.pallas import tpu as pltpu
from jax.sharding import PartitionSpec as P

MESH = pl.DeviceIdType.MESH
Q = 2
W = 128
B = 256
OWN, NEXT = 0, 1


def device(x, zl, core, zh, y):
    return ((x * 4 + zl) * 2 + core, zh * 4 + y)


def differ(a, b):
    return a + b - 2 * a * b


def split(value):
    high = value.astype(jnp.bfloat16)
    return high, (value - high.astype(jnp.float32)).astype(jnp.bfloat16)


def dot3(a_high, a_low, b_high, b_low):
    dot = functools.partial(jnp.dot, preferred_element_type=jnp.float32)
    return dot(a_high, b_high) + (dot(a_high, b_low) + dot(a_low, b_high))


def kernel(
    a_ref, m_ref, st_ref, dinv_ref, p_ref, d_ref,
    a_own, a_mate, a_next, a_far, a_hi, a_lo, m_in, m_own, mt_hi, mt_lo, m_all, m_hi, m_lo,
    part, c1, c2, nf, t_buf, t_in, z_in, t_out, dinv,
    load_sem, am_sem, an_s, an_r, af_s, af_r, home_s, home_r, z_s, z_r, x_s, x_r, f_s, f_r,
    e1_s, c1_r, o_s, c2_r, n_s, n_r, ds_s, ds_r, dz_s, dz_r, dg_s, dg_r,
):
    row = lax.axis_index("row")
    col = lax.axis_index("col")
    x, zl, core = row // 8, (row // 2) % 4, row % 2
    zh, y = col // 4, col % 4
    t, s = zl // 2, zl % 2

    load_m = pltpu.make_async_copy(m_ref, m_in, load_sem.at[0])
    load_m.start()
    load_a = pltpu.make_async_copy(a_ref, a_own, load_sem.at[1])
    load_a.start()
    load_d = pltpu.make_async_copy(dinv_ref, dinv, load_sem.at[2])
    load_d.start()

    to_zh, to_y = x // 2, (x % 2) * 2 + t
    turn = differ(zh, to_zh) * differ(t, zh)
    to_x = (2 * core + y // 2 + x) % 4
    to_zl = 2 * differ(s, turn) + zh
    home = device(to_x, to_zl, y % 2, to_zh, to_y)
    off = (
        (to_x - x) * (to_x - x) + (to_zl - zl) * (to_zl - zl) + (y % 2 - core) * (y % 2 - core)
        + (to_zh - zh) * (to_zh - zh) + (to_y - y) * (to_y - y)
    )
    from_x = 2 * zh + y // 2
    turned = differ(s, zh) * differ(y % 2, s)

    def block_of(at_x, at_t):
        m = (at_x - from_x + 8) % 4
        return 2 * differ(at_t, turned) + m // 2, m % 2

    def unit(q, at_x, at_t):
        j, i = block_of(at_x, at_t)
        return m_all.at[q, j, i]

    j_here, i_here = block_of(x, t)
    source = device(from_x, 2 * (y % 2) + j_here // 2, j_here % 2, s, 2 * i_here + core)

    even = 1 - differ(core, y % 2)
    apart = differ(zh, s)
    right_y, left_y = (y + 1) % 4, (y + 3) % 4
    right, left = (row, zh * 4 + right_y), (row, zh * 4 + left_y)
    mate = device(x, zl, 1 - core, zh, y)
    nextz = device(x, 2 * t + 1 - s, core, zh, y)
    me = x * 2 + core

    barrier = pltpu.get_barrier_semaphore()

    def greet(target):
        pl.semaphore_signal(barrier, inc=1, device_id=target, device_id_type=MESH)

    def peer_x(e):
        return device(e // 2, zl, e % 2, zh, y)

    for d in range(1, 8):
        greet(peer_x((me + d) % 8))
    for d in range(1, 4):
        greet(device(x, (zl + d) % 4, core, zh, y))
    greet(right)
    greet(left)
    near_from = device(x, 2 * t + zh, y % 2, zh, y)
    far_from = device(x, 2 * t + zh, y % 2, 1 - zh, y)
    greet(far_from)
    near_self = (1 - differ(s, zh)) * even

    @pl.when(near_self == 0)
    def _():
        greet(near_from)

    @pl.when(off > 0)
    def _():
        greet(source)

    listed = st_ref[0, 0] == row
    for k in range(1, 16):
        listed = listed | (st_ref[0, k] == row)
    keep = jnp.where(listed, 1, 0)
    load_m.wait()
    masked = jnp.where(jnp.broadcast_to(keep, (B, B)) > 0, m_in[...], 0.0)
    for q in range(Q):
        m_own[q] = masked[:, q * W:(q + 1) * W]

    pl.semaphore_wait(barrier, 12 + jnp.minimum(off, 1) + even * (4 * apart + 3 * (1 - apart)))

    def remote(src, dst, send, recv, target):
        return pltpu.make_async_remote_copy(
            src_ref=src, dst_ref=dst, send_sem=send, recv_sem=recv,
            device_id=target, device_id_type=MESH,
        )

    sends = []

    def launch(*args):
        copy = remote(*args)
        copy.start()
        sends.append(copy)

    def arrived(buf, recv):
        remote(buf, buf, load_sem.at[0], recv, mate).wait_recv()

    slot_j, slot_i = 2 * s + core, y // 2

    def home_copy(q):
        return remote(m_own.at[q], m_all.at[q, slot_j, slot_i], home_s.at[q], home_r.at[q], home)

    def home_send(q):
        @pl.when(off > 0)
        def _():
            home_copy(q).start()

        @pl.when(off == 0)
        def _():
            pltpu.make_async_copy(m_own.at[q], m_all.at[q, slot_j, slot_i], home_r.at[q]).start()

    def home_left(q):
        @pl.when(off > 0)
        def _():
            home_copy(q).wait_send()

    def next_send(j):
        launch(a_ref.at[:, j * B:(j + 1) * B], a_next.at[j], an_s.at[j], an_r.at[j], nextz)

    def next_pass(j):
        arrived(a_next.at[j], an_r.at[j])
        launch(a_next.at[j], a_far.at[j], af_s.at[j], af_r.at[j], mate)

    home_send(0)
    home_send(1)
    launch(a_ref, a_mate, am_sem.at[0], am_sem.at[1], mate)

    def strip(pair, c):
        return 2 * (s if pair == OWN else 1 - s) + c

    mt_hi[...], mt_lo[...] = split(masked.T)
    load_a.wait()
    a_hi[strip(OWN, core)], a_lo[strip(OWN, core)] = split(a_own[...])

    def z_send(q):
        launch(unit(q, x, t), unit(q, x, t), z_s.at[q], z_r.at[q],
               device(x, (zl + 2) % 4, core, zh, y))

    def x_send(q, a):
        u = unit(q, x, differ(t, a))
        for i, d in enumerate((1, 3)):
            launch(u, u, x_s.at[q, a, i], x_r.at[q, a, i], device((x + d) % 4, zl, core, zh, y))

    def x_arrived(q, a, i):
        arrived(unit(q, x + (3 if i == 0 else 1), differ(t, a)), x_r.at[q, a, i])

    def forward(q):
        for a in range(2):
            x_arrived(q, a, a)
            u = unit(q, x + (3 if a == 0 else 1), differ(t, a))
            launch(u, u, f_s.at[q, a], f_r.at[q, a],
                   device((x + (1 if a == 0 else 3)) % 4, zl, core, zh, y))

    def gathered(q):
        for a in range(2):
            x_arrived(q, a, 1 - a)
        for a in range(2):
            arrived(unit(q, x + 2, differ(t, a)), f_r.at[q, a])
        for j in range(4):
            for i in range(2):
                rows, cols = slice(j * B, (j + 1) * B), slice(i * W, (i + 1) * W)
                m_hi[q, rows, cols], m_lo[q, rows, cols] = split(m_all[q, j, i])

    def home_arrived(q):
        u = unit(q, x, t)
        pltpu.make_async_copy(u, u, home_r.at[q]).wait()

    def multiply(q, pair):
        for c in range(2):
            r = strip(pair, c)
            out = dot3(a_hi[r], a_lo[r], m_hi[q], m_lo[q])
            for i in range(2):
                part[q, r, i] = out[:, i * W:(i + 1) * W]

    over, at_right, at_left, here = ((y + 2) % 4) // 2, right_y // 2, left_y // 2, y // 2

    def first_even(q, pair):
        return (
            remote(part.at[q, strip(pair, 0), over], c1.at[q, pair, 0], e1_s.at[q, pair, 0],
                   c1_r.at[q, pair, 0], right),
            remote(part.at[q, strip(pair, 1), over], c1.at[q, pair, 1], e1_s.at[q, pair, 1],
                   c1_r.at[q, pair, 1], left),
        )

    def to_sum(q, pair, i, c):
        return remote(part.at[q, strip(pair, c), at_right if i == 0 else at_left],
                      c2.at[q, pair, i, c], o_s.at[q, pair, i, c], c2_r.at[q, pair, i, c],
                      right if i == 0 else left)

    def scatter_first(q, pair):
        @pl.when(even == 1)
        def _():
            for copy in first_even(q, pair):
                copy.start()

        @pl.when(even == 0)
        def _():
            to_sum(q, pair, 0, 1).start()
            to_sum(q, pair, 1, 0).start()

    def scatter_second(q, pair):
        @pl.when(even == 0)
        def _():
            for i in range(2):
                arrived(c1.at[q, pair, i], c1_r.at[q, pair, i])
                r, k = strip(pair, i), at_right if i == 0 else at_left
                part[q, r, k] = part[q, r, k] + c1[q, pair, i]
                to_sum(q, pair, i, i).start()

    def to_owner(q, pair, c):
        zl_to = 2 * t + (s if pair == OWN else 1 - s)
        return remote(part.at[q, strip(pair, c), here], nf.at[q, apart], n_s.at[q, pair, c],
                      n_r.at[q, apart], device(x, zl_to, c, s, y))

    def is_self(pair, c):
        if pair == NEXT:
            return None
        return (1 - apart) * (1 - differ(core, c))

    def scatter_last(q, pair):
        @pl.when(even == 1)
        def _():
            for c in range(2):
                for i in range(2):
                    arrived(c2.at[q, pair, i, c], c2_r.at[q, pair, i, c])
                r = strip(pair, c)
                part[q, r, here] = part[q, r, here] + (c2[q, pair, 0, c] + c2[q, pair, 1, c])
                local = is_self(pair, c)
                if local is None:
                    to_owner(q, pair, c).start()
                else:
                    @pl.when(local == 0)
                    def _():
                        to_owner(q, pair, c).start()

                    @pl.when(local == 1)
                    def _():
                        pltpu.make_async_copy(
                            part.at[q, r, here], nf.at[q, 0], n_r.at[q, 0]
                        ).start()

    def slice_copy(q, d):
        e = (me + d) % 8
        return remote(t_buf.at[q, e], t_in.at[q, me], ds_s.at[q, d], ds_r.at[q], peer_x(e))

    def sum_copy(q, d):
        return remote(z_in.at[q, zl], z_in.at[q, zl], dz_s.at[q, d], dz_r.at[q],
                      device(x, (zl + d) % 4, core, zh, y))

    def result_copy(q, d):
        return remote(t_out.at[q, me], t_out.at[q, me], dg_s.at[q, d], dg_r.at[q],
                      peer_x((me + d) % 8))

    def finish(q):
        for i in range(2):
            pltpu.make_async_copy(nf.at[q, i], nf.at[q, i], n_r.at[q, i]).wait()
        total = nf[q, 0] + nf[q, 1]
        panel = jnp.where(jnp.broadcast_to(keep, (B, W)) > 0, -total, 0.0)
        p_ref[:, q * W:(q + 1) * W] = panel
        p_hi, p_lo = split(panel)
        t_buf[q] = dot3(mt_hi[...], mt_lo[...], p_hi, p_lo).reshape(8, 32, W)
        for d in range(1, 8):
            slice_copy(q, d).start()
        t_in[q, me] = t_buf[q, me]

    def diagonal_sum(q):
        arrived(t_in.at[q, pl.ds(0, 7)], ds_r.at[q])
        z_in[q, zl] = jnp.sum(t_in[q], axis=0)
        for d in range(1, 4):
            sum_copy(q, d).start()

    def diagonal_share(q):
        arrived(z_in.at[q, pl.ds(0, 3)], dz_r.at[q])
        first = pl.multiple_of(me * 32, 32)
        t_out[q, me] = dinv[pl.ds(first, 32), q * W:(q + 1) * W] - jnp.sum(z_in[q], axis=0)
        for d in range(1, 8):
            result_copy(q, d).start()

    def diagonal_store(q):
        arrived(t_out.at[q, pl.ds(0, 7)], dg_r.at[q])
        d_ref[:, q * W:(q + 1) * W] = t_out[q].reshape(B, W)

    next_send(0)
    home_arrived(0)
    z_send(0)
    x_send(0, 0)
    next_send(1)
    home_left(0)
    home_left(1)
    arrived(unit(0, x, 1 - t), z_r.at[0])
    x_send(0, 1)
    next_send(2)
    arrived(a_mate, am_sem.at[1])
    a_hi[strip(OWN, 1 - core)], a_lo[strip(OWN, 1 - core)] = split(a_mate[...])
    home_arrived(1)
    z_send(1)
    x_send(1, 0)
    next_send(3)
    forward(0)
    arrived(unit(1, x, 1 - t), z_r.at[1])
    x_send(1, 1)
    next_pass(0)
    next_pass(1)
    gathered(0)
    multiply(0, OWN)
    scatter_first(0, OWN)
    forward(1)
    next_pass(2)
    scatter_second(0, OWN)
    next_pass(3)
    for j in range(4):
        cols = slice(j * B, (j + 1) * B)
        r = strip(NEXT, core)
        a_hi[r, :, cols], a_lo[r, :, cols] = split(a_next[j])
        arrived(a_far.at[j], af_r.at[j])
        r = strip(NEXT, 1 - core)
        a_hi[r, :, cols], a_lo[r, :, cols] = split(a_far[j])
    multiply(0, NEXT)
    scatter_first(0, NEXT)
    scatter_last(0, OWN)
    gathered(1)
    multiply(1, OWN)
    scatter_first(1, OWN)
    scatter_second(0, NEXT)
    multiply(1, NEXT)
    scatter_first(1, NEXT)
    scatter_second(1, OWN)
    scatter_last(0, NEXT)
    scatter_second(1, NEXT)
    load_d.wait()
    scatter_last(1, OWN)
    finish(0)
    scatter_last(1, NEXT)
    diagonal_sum(0)
    finish(1)
    diagonal_share(0)
    diagonal_sum(1)
    diagonal_store(0)
    for copy in sends:
        copy.wait_send()
    for q in range(Q):
        @pl.when(even == 1)
        def _(q=q):
            for pair in range(2):
                for copy in first_even(q, pair):
                    copy.wait_send()
                for c in range(2):
                    local = is_self(pair, c)
                    if local is None:
                        to_owner(q, pair, c).wait_send()
                    else:
                        @pl.when(local == 0)
                        def _():
                            to_owner(q, pair, c).wait_send()

        @pl.when(even == 0)
        def _(q=q):
            for pair in range(2):
                for i in range(2):
                    for c in range(2):
                        to_sum(q, pair, i, c).wait_send()

    def diagonal_left(q):
        for d in range(1, 8):
            slice_copy(q, d).wait_send()
        for d in range(1, 4):
            sum_copy(q, d).wait_send()

    def shared(q):
        for d in range(1, 8):
            result_copy(q, d).wait_send()

    diagonal_share(1)
    diagonal_left(0)
    diagonal_left(1)
    shared(0)
    diagonal_store(1)
    shared(1)


def local(inverse_anc, lower_panel, structure, diag_inverse):
    f32, bf16 = jnp.float32, jnp.bfloat16
    dma = pltpu.SemaphoreType.DMA
    hbm = pl.BlockSpec(memory_space=pl.ANY)
    vmem = pl.BlockSpec(memory_space=pltpu.VMEM)
    return pl.pallas_call(
        kernel,
        out_shape=(jax.ShapeDtypeStruct((B, B), f32), jax.ShapeDtypeStruct((B, B), f32)),
        in_specs=[hbm, hbm, pl.BlockSpec(memory_space=pltpu.SMEM), hbm],
        out_specs=(vmem, vmem),
        scratch_shapes=[
            pltpu.VMEM((B, 4 * B), f32), pltpu.VMEM((B, 4 * B), f32),
            pltpu.VMEM((4, B, B), f32), pltpu.VMEM((4, B, B), f32),
            pltpu.VMEM((4, B, 4 * B), bf16), pltpu.VMEM((4, B, 4 * B), bf16),
            pltpu.VMEM((B, B), f32), pltpu.VMEM((Q, B, W), f32),
            pltpu.VMEM((B, B), bf16), pltpu.VMEM((B, B), bf16),
            pltpu.VMEM((Q, 4, 2, B, W), f32),
            pltpu.VMEM((Q, 4 * B, 2 * W), bf16), pltpu.VMEM((Q, 4 * B, 2 * W), bf16),
            pltpu.VMEM((Q, 4, 2, B, W), f32),
            pltpu.VMEM((Q, 2, 2, B, W), f32), pltpu.VMEM((Q, 2, 2, 2, B, W), f32),
            pltpu.VMEM((Q, 2, B, W), f32),
            pltpu.VMEM((Q, 8, 32, W), f32), pltpu.VMEM((Q, 8, 32, W), f32),
            pltpu.VMEM((Q, 4, 32, W), f32), pltpu.VMEM((Q, 8, 32, W), f32),
            pltpu.VMEM((B, B), f32),
            dma((3,)), dma((2,)), dma((4,)), dma((4,)), dma((4,)), dma((4,)),
            dma((Q,)), dma((Q,)), dma((Q,)), dma((Q,)),
            dma((Q, 2, 2)), dma((Q, 2, 2)), dma((Q, 2)), dma((Q, 2)),
            dma((Q, 2, 2)), dma((Q, 2, 2)), dma((Q, 2, 2, 2)), dma((Q, 2, 2, 2)),
            dma((Q, 2, 2)), dma((Q, 2)),
            dma((Q, 8)), dma((Q,)), dma((Q, 4)), dma((Q,)), dma((Q, 8)), dma((Q,)),
        ],
        compiler_params=pltpu.CompilerParams(
            collective_id=0, has_side_effects=True, vmem_limit_bytes=62 * 2**20
        ),
    )(inverse_anc, lower_panel, structure, diag_inverse)


def solution(mesh):
    placed = (P("row", "col"), P("row", "col"), P("col", None), P("col", None))
    return jax.shard_map(
        local,
        mesh=mesh,
        in_specs=placed,
        out_specs=(P("row", "col"), P("col", None)),
        check_vma=False,
    )
```

time: 639 us -> 98.9 us (0.15)
  waiting for transfers between devices: 605 us -> 0 us
  Pallas kernels: 0 us -> 95.6 us
  matrix products: 13.7 us -> 0 us
  between operations: 13.8 us -> 0.65 us
    psum x1 -> x0, waiting for transfers between devices: 274 us -> none  [local(): lax.psum(partial_value.reshape(local_count * sn_width, sn_width), 'row')]
    all_gather x1 -> x0, waiting for transfers between devices: 178 us -> none  [local(): strip = lax.all_gather(inverse_anc, 'col', axis=1, tiled=True)]
    reduce_scatter x1 -> x0, waiting for transfers between devices: 153 us -> none  [local(): lax.psum_scatter(lax.dot_general(strip, masked, (((0,), (0,)), ((), ())),...]
    pallas_call x0 -> x1, Pallas kernels: none -> 95.6 us  [local(): pl.pallas_call(kernel, out_shape=(jax.ShapeDtypeStruct((B, B), f32), jax....]
    dot_general x2 -> x0, matrix products: 13.7 us -> none  [the longest x1 11.7 us: local(): lax.dot_general(strip, masked, (((0,), (0,)), ((), ())), precision=lax.Pr...]
  transfers between devices with their start and end apart: 3 -> 0, of which waited for: 3 -> 0; matrix products, arithmetic and copies ran while one was open for 1% -> 0% of each run, Pallas kernels for 0% -> 0%
where the time goes in v2:
time: 98.9 us; the launch traced here: 98.6 us
  Pallas kernels  95.6 us (97%)
  local copies, waits for them, and re-layouts  2.42 us (2%)
    pallas_call x1, Pallas kernels, local(): pl.pallas_call(kernel, out_shape=(jax.ShapeDtypeStruct((B, B), f32), jax....  95.6 us
    unnamed x4, local copies, waits for them, and re-layouts  2.42 us

profile of v2, /device:TPU:1, one launch (start us, length us, event | category | flops | bytes accessed | tf_op | source)
XLA Modules:
  0.0 98.6 jit_solution(7059527592869671200)
XLA Ops:
  0.6 95.6 %shard_map.59 = (f32[256,256]{1,0:T(8,128)}, f32[256,256]{1,0:T(8,128)}) custom-call(f32[256,1024]{1,0:T(8,128)} %a_ref.1, f32[256,256]{1,0:T(8,128)} %m_ref.1, s32[1,16]{1,0:T(1,128)} %st_ref.1, f32[256,256]{1,0:T(8,128)} %dinv_ref.1), custom_call_target="tpu_custom_call" | custom-call | tf_op jit(solution)/shard_map/pallas_call | solution.py:428
  96.2 0.0 copy-start
  96.2 1.7 %copy.8 = f32[256,256]{1,0:T(8,128)} copy(f32[256,256]{1,0:T(8,128)} %get-tuple-element.4) | data formatting | bytes 524288
  97.9 0.0 copy-done
  97.9 0.7 copy.9
Async XLA Ops:
  96.2 1.7 %copy-start = (f32[256,256]{1,0:T(8,128)S(1)}, f32[256,256]{1,0:T(8,128)}, u32[]{:S(2)}) copy-start(f32[256,256]{1,0:T(8,128)} %get-tuple-element.5) | copy-start | bytes 786436

commit v3 on v2

--- a/solution.py
+++ b/solution.py
@@ -332,8 +332,6 @@
     arrived(unit(0, x, 1 - t), z_r.at[0])
     x_send(0, 1)
     next_send(2)
-    arrived(a_mate, am_sem.at[1])
-    a_hi[strip(OWN, 1 - core)], a_lo[strip(OWN, 1 - core)] = split(a_mate[...])
     home_arrived(1)
     z_send(1)
     x_send(1, 0)
@@ -341,6 +339,8 @@
     forward(0)
     arrived(unit(1, x, 1 - t), z_r.at[1])
     x_send(1, 1)
+    arrived(a_mate, am_sem.at[1])
+    a_hi[strip(OWN, 1 - core)], a_lo[strip(OWN, 1 - core)] = split(a_mate[...])
     next_pass(0)
     next_pass(1)
     gathered(0)
@@ -371,8 +371,8 @@
     scatter_second(1, NEXT)
     load_d.wait()
     scatter_last(1, OWN)
+    scatter_last(1, NEXT)
     finish(0)
-    scatter_last(1, NEXT)
     diagonal_sum(0)
     finish(1)
     diagonal_share(0)

time: 98.9 us -> 96.7 us (0.978)
  Pallas kernels: 95.6 us -> 93.5 us
    pallas_call x1, Pallas kernels: 95.6 us -> 93.5 us  [local(): pl.pallas_call(kernel, out_shape=(jax.ShapeDtypeStruct((B, B), f32), jax....]
where the time goes in v3:
time: 96.7 us; the launch traced here: 96.6 us
  Pallas kernels  93.5 us (97%)
  local copies, waits for them, and re-layouts  2.42 us (3%)
    pallas_call x1, Pallas kernels, local(): pl.pallas_call(kernel, out_shape=(jax.ShapeDtypeStruct((B, B), f32), jax....  93.5 us
    unnamed x4, local copies, waits for them, and re-layouts  2.42 us

profile of v3, /device:TPU:1, one launch (start us, length us, event | category | flops | bytes accessed | tf_op | source)
XLA Modules:
  0.0 96.6 jit_solution(9816729847743789580)
XLA Ops:
  0.6 93.5 %shard_map.59 = (f32[256,256]{1,0:T(8,128)}, f32[256,256]{1,0:T(8,128)}) custom-call(f32[256,1024]{1,0:T(8,128)} %a_ref.1, f32[256,256]{1,0:T(8,128)} %m_ref.1, s32[1,16]{1,0:T(1,128)} %st_ref.1, f32[256,256]{1,0:T(8,128)} %dinv_ref.1), custom_call_target="tpu_custom_call" | custom-call | tf_op jit(solution)/shard_map/pallas_call | solution.py:428
  94.2 0.0 copy-start
  94.2 1.7 %copy.8 = f32[256,256]{1,0:T(8,128)} copy(f32[256,256]{1,0:T(8,128)} %get-tuple-element.4) | data formatting | bytes 524288
  95.9 0.0 copy-done
  95.9 0.7 copy.9
Async XLA Ops:
  94.2 1.7 %copy-start = (f32[256,256]{1,0:T(8,128)S(1)}, f32[256,256]{1,0:T(8,128)}, u32[]{:S(2)}) copy-start(f32[256,256]{1,0:T(8,128)} %get-tuple-element.5) | copy-start | bytes 786436

commit v4 on v3

--- a/solution.py
+++ b/solution.py
@@ -207,6 +207,17 @@
         u = unit(q, x, t)
         pltpu.make_async_copy(u, u, home_r.at[q]).wait()
 
+    def split_next(j):
+        cols = slice(j * B, (j + 1) * B)
+        r = strip(NEXT, core)
+        a_hi[r, :, cols], a_lo[r, :, cols] = split(a_next[j])
+
+    def split_far(j):
+        arrived(a_far.at[j], af_r.at[j])
+        cols = slice(j * B, (j + 1) * B)
+        r = strip(NEXT, 1 - core)
+        a_hi[r, :, cols], a_lo[r, :, cols] = split(a_far[j])
+
     def multiply(q, pair):
         for c in range(2):
             r = strip(pair, c)
@@ -301,7 +312,7 @@
         p_ref[:, q * W:(q + 1) * W] = panel
         p_hi, p_lo = split(panel)
         t_buf[q] = dot3(mt_hi[...], mt_lo[...], p_hi, p_lo).reshape(8, 32, W)
-        for d in range(1, 8):
+        for d in (4, 3, 5, 2, 6, 7, 1):
             slice_copy(q, d).start()
         t_in[q, me] = t_buf[q, me]
 
@@ -315,7 +326,7 @@
         arrived(z_in.at[q, pl.ds(0, 3)], dz_r.at[q])
         first = pl.multiple_of(me * 32, 32)
         t_out[q, me] = dinv[pl.ds(first, 32), q * W:(q + 1) * W] - jnp.sum(z_in[q], axis=0)
-        for d in range(1, 8):
+        for d in (4, 3, 5, 2, 6, 7, 1):
             result_copy(q, d).start()
 
     def diagonal_store(q):
@@ -349,14 +360,14 @@
     forward(1)
     next_pass(2)
     scatter_second(0, OWN)
+    for j in range(3):
+        split_next(j)
+    split_far(0)
+    split_far(1)
     next_pass(3)
-    for j in range(4):
-        cols = slice(j * B, (j + 1) * B)
-        r = strip(NEXT, core)
-        a_hi[r, :, cols], a_lo[r, :, cols] = split(a_next[j])
-        arrived(a_far.at[j], af_r.at[j])
-        r = strip(NEXT, 1 - core)
-        a_hi[r, :, cols], a_lo[r, :, cols] = split(a_far[j])
+    split_far(2)
+    split_next(3)
+    split_far(3)
     multiply(0, NEXT)
     scatter_first(0, NEXT)
     scatter_last(0, OWN)

time: 96.7 us -> 96.4 us (level)
  no operation moved by 1% of the time
where the time goes in v4:
time: 96.4 us; the launch traced here: 96.3 us
  Pallas kernels  93.2 us (97%)
  local copies, waits for them, and re-layouts  2.42 us (3%)
    pallas_call x1, Pallas kernels, local(): pl.pallas_call(kernel, out_shape=(jax.ShapeDtypeStruct((B, B), f32), jax....  93.2 us
    unnamed x4, local copies, waits for them, and re-layouts  2.42 us

profile of v4, /device:TPU:1, one launch (start us, length us, event | category | flops | bytes accessed | tf_op | source)
XLA Modules:
  0.0 96.3 jit_solution(2140961633918033051)
XLA Ops:
  0.6 93.2 %shard_map.59 = (f32[256,256]{1,0:T(8,128)}, f32[256,256]{1,0:T(8,128)}) custom-call(f32[256,1024]{1,0:T(8,128)} %a_ref.1, f32[256,256]{1,0:T(8,128)} %m_ref.1, s32[1,16]{1,0:T(1,128)} %st_ref.1, f32[256,256]{1,0:T(8,128)} %dinv_ref.1), custom_call_target="tpu_custom_call" | custom-call | tf_op jit(solution)/shard_map/pallas_call | solution.py:439
  93.9 0.0 copy-start
  93.9 1.7 %copy.8 = f32[256,256]{1,0:T(8,128)} copy(f32[256,256]{1,0:T(8,128)} %get-tuple-element.4) | data formatting | bytes 524288
  95.6 0.0 copy-done
  95.6 0.7 copy.9
Async XLA Ops:
  93.9 1.7 %copy-start = (f32[256,256]{1,0:T(8,128)S(1)}, f32[256,256]{1,0:T(8,128)}, u32[]{:S(2)}) copy-start(f32[256,256]{1,0:T(8,128)} %get-tuple-element.5) | copy-start | bytes 786436
